TPU v7x, 768 devices: a whole 4x8x12 slice. The times are simulated.
768 devices in a mesh: row: 32 (over z_hi, x, core), col: 24 (over z_lo, y).
Axes of the slice: x: 4, y: 8, z: 12 (z_hi: 4, z_lo: 3; z = z_hi * 3 + z_lo), core: 2. Of those that a mesh axis runs over, the one named last changes fastest.
Arguments:
- u_blocks: float32 [96, 168, 128, 128], P('row', 'col'), may hold values from -0.21875 to 0.21875
- u_rows: int32 [96, 168], P('row', 'col'), may hold values from 0 to 2
Outputs:
- squares: float32 [128, 72, 3, 128, 128], P('row', 'col')
All inputs are finite; a program needn't handle non-finite values.
Results may differ from a plain program's by a relative error of at most 0.0001.
Values sent between devices are 32-bit elements; how exact they have to be, the bound alone decides.
A program may use at most 32 MiB of HBM per device.

v0:
```python
import functools

import jax
import jax.numpy as jnp
from jax import lax
from jax.experimental import pallas as pl
from jax.experimental.pallas import tpu as pltpu
from jax.sharding import PartitionSpec as P

MESH = pl.DeviceIdType.MESH
BS = 128
TAU = 3
STEPS = 4
N_ROW = 32
N_COL = 24
HEIGHT = BS + 8

RING = 8


def straight(k, m):
    return (
        lambda r, c: ((r + N_ROW - k) % N_ROW, (c + N_COL - m) % N_COL),
        lambda r, c: ((r + N_ROW + k) % N_ROW, (c + N_COL + m) % N_COL),
    )


def around(at, k):
    return at - at % RING + (at % RING + RING - k) % RING


def in_plane(k, m):
    return lambda r, c: (around(r, k), around(c, m)), lambda r, c: (around(r, -k), around(c, -m))


def in_row_plane(k, m):
    return (
        lambda r, c: (around(r, k), (c + N_COL - m) % N_COL),
        lambda r, c: (around(r, -k), (c + m) % N_COL),
    )


def wrapped(at, k):
    return jnp.where(at % RING >= RING - k, RING, 0)


def down(k, m):
    return (
        lambda r, c: ((r + N_ROW - wrapped(r, k)) % N_ROW, (c + N_COL - wrapped(c, m)) % N_COL),
        lambda r, c: ((r + wrapped(r, k)) % N_ROW, (c + wrapped(c, m)) % N_COL),
    )


class Leg:
    def __init__(self, name, src, move, sends=None):
        self.name, self.src, self.sends, self.after = name, src, sends, AFTER.get(name)
        self.to, self.origin = move
        self.gets = None if sends is None else lambda r, c: sends(*self.origin(r, c))


def plan():
    legs, final = {}, {}

    def leg(name, src, move, sends=None):
        legs[name] = Leg(name, src, move, sends)
        return name

    def late(name, src, k, m):
        crossed = lambda r, c: (r % RING >= RING - k) | (c % RING >= RING - m)
        leg(name, src, in_plane(k, m))
        leg(name + "z", name, down(k, m), crossed)
        return crossed, name + "z", name

    low = lambda k: lambda r, c: r % RING < k
    rows = lambda a, b: lambda r, c: (r % RING >= a) & (r % RING < b)
    wide = lambda r, c: c % RING >= 4

    leg("f3", "F3", straight(RING, 0), low(6))
    leg("fe3", (low(6), "f3", "F3"), in_plane(6, 0))
    leg("fm3", (low(3), "f3", "F3"), in_row_plane(3, 3))
    bs3 = leg("bs3", "B3", straight(0, 6))
    leg("bm3", bs3, straight(3, -3))
    final[3] = "fm3", bs3, "fe3", "bm3"

    leg("f2", "F2", straight(RING, 0), rows(2, 4))
    leg("fe2", (rows(2, 4), "f2", "F2"), in_plane(4, 0))
    leg("fe2z", "fe2", straight(RING, 0), rows(4, 6))
    leg("fm2", "F2", in_row_plane(2, 2), rows(2, 8))
    leg("fm2x", "fe2z", in_row_plane(-2, 2), rows(4, 6))
    leg("p2", "B2", in_plane(0, -2))
    leg("bs2", "p2", in_plane(0, -2))
    leg("bs2z", "bs2", down(0, 4), wide)
    bm2 = late("bm2", "B2", 2, 2)
    final[2] = (rows(6, 8), "fm2x", "fm2"), (wide, "bs2z", "bs2"), (rows(4, 6), "fe2z", "fe2"), bm2

    n1 = late("n1", "F1", 1, 0)
    c1 = leg("c1", "B1", straight(0, 1))
    fe1 = late("fe1", n1, 1, 0)
    fm1 = late("fm1", n1, 0, 1)
    leg("bm1", c1, straight(1, 0))
    leg("bs1", c1, straight(0, 1))
    final[1] = fm1, "bs1", fe1, "bm1"

    return [legs[name] for name in ORDER], final


ORDER = (
    "n1", "n1z", "fe1", "p2", "f3", "f2", "bs3", "fe1z", "fm1", "fe2", "fe2z", "fe3", "bm2", "c1", "bs2", "bm1",
    "fm3", "bm2z", "fm1z", "bs1", "fm2", "fm2x", "bs2z", "bm3",
)
AFTER = {"bm2": "n1", "c1": "f2", "fe2": "fe1", "fm3": "f2", "p2": "n1"}


OWN = ["F1", "F2", "F3", "B1", "B2", "B3"]


def places(legs):
    return {name: at for at, name in enumerate(OWN + [leg.name for leg in legs])}


def pick(src, at, r, c):
    if isinstance(src, str):
        return at[src]
    condition, yes, no = src
    return jnp.where(condition(r, c), at[yes], at[no])


def names(src):
    return {src} if isinstance(src, str) else set(src[1:])


def when(condition, r, c, do):
    if condition is None:
        do()
    else:
        pl.when(condition(r, c))(do)


def split(value):
    high = value.astype(jnp.bfloat16)
    return high, (value - high.astype(jnp.float32)).astype(jnp.bfloat16)


def dot(a, b):
    return jnp.dot(a, b, preferred_element_type=jnp.float32)


def kernel(legs, final, u_ref, rows_hbm, out_ref, buf, onsite, rows_ref, sides, rows_sem, load_sem, send_sem, recv_sem):
    r, c = lax.axis_index("row"), lax.axis_index("col")
    at = places(legs)
    copies = {}
    for number, leg in enumerate(legs):
        copies[leg.name] = pltpu.make_async_remote_copy(
            src_ref=buf.at[pick(leg.src, at, r, c)],
            dst_ref=buf.at[at[leg.name]],
            send_sem=send_sem.at[number],
            recv_sem=recv_sem.at[number],
            device_id=leg.to(r, c),
            device_id_type=MESH,
        )

    barrier = pltpu.get_barrier_semaphore()
    partners = 0
    for leg in legs:
        greet = functools.partial(
            pl.semaphore_signal, barrier, inc=1, device_id=leg.origin(r, c), device_id_type=MESH
        )
        when(leg.gets, r, c, greet)
        partners += 1 if leg.sends is None else jnp.where(leg.sends(r, c), 1, 0)

    loads = [pltpu.make_async_copy(rows_hbm, rows_ref, rows_sem)]
    loads[0].start()
    for j in range(2 * STEPS - 1):
        for t in range(TAU):
            target = onsite.at[t] if j == 0 else buf.at[j - 1, t, pl.ds(0, BS)]
            loads.append(pltpu.make_async_copy(u_ref.at[t, j], target, load_sem.at[j, t]))
            loads[-1].start()
    loads[0].wait()
    for j in range(1, 2 * STEPS - 1):
        for t in range(TAU):
            buf[j - 1, t, BS:HEIGHT, :] = jnp.full((HEIGHT - BS, BS), rows_ref[t, j], jnp.int32).astype(jnp.float32)
    for load in loads[1:]:
        load.wait()
    pl.semaphore_wait(barrier, partners)

    rank = {None: -1, **{leg.name: number for number, leg in enumerate(legs)}}

    def trigger(leg, source):
        return max(None if source in OWN else source, leg.after, key=rank.get)

    def begin(event):
        for leg in legs:
            go = copies[leg.name].start
            if isinstance(leg.src, str):
                if event == trigger(leg, leg.src):
                    when(leg.sends, r, c, go)
            else:
                condition, yes, no = leg.src
                if event == trigger(leg, yes):
                    when(condition, r, c, go)
                if event == trigger(leg, no):
                    when(lambda r, c: jnp.logical_not(condition(r, c)), r, c, go)

    begin(None)

    def put(side, i, k, value):
        high, low = split(value)
        side[0, i * BS : (i + 1) * BS, k * BS : (k + 1) * BS] = high
        side[1, i * BS : (i + 1) * BS, k * BS : (k + 1) * BS] = low

    def chosen(label, k, block):
        return jnp.where(label == float(k), block, 0.0)

    def assemble(side, forward, forward_labels, backward, backward_labels):
        for i in range(TAU):
            turned = backward(i).T
            for k in range(TAU):
                put(side, i, k, chosen(forward_labels(k), i, forward(k)) + chosen(backward_labels(i), k, turned))

    def multiply(s, left, right):
        for i in range(TAU):
            rows = slice(i * BS, (i + 1) * BS)
            high = left[0, rows, :]
            total = dot(high, right[1]) + dot(left[1, rows, :], right[0]) + dot(high, right[0])
            for j in range(TAU):
                out_ref[s, i, j] = total[:, j * BS : (j + 1) * BS]

    def form_onsite():
        labels = lambda t: jnp.full((1, BS), rows_ref[t, 0], jnp.int32).astype(jnp.float32)
        block = lambda t: onsite[t]
        side = sides.at[0, 0]
        assemble(side, block, labels, block, labels)
        multiply(0, side, side)

    def parts_of(src):
        place = pick(src, at, r, c)
        block = lambda t: buf[place, t, :BS, :]
        labels = lambda t: buf[place, t, BS : BS + 1, :]
        return block, labels

    arrived, formed = set(OWN), set()
    passing = max(number for number, leg in enumerate(legs) for later in legs if leg.name in names(later.src) | {later.after})
    for number, leg in enumerate(legs):
        when(leg.gets, r, c, copies[leg.name].wait_recv)
        arrived.add(leg.name)
        begin(leg.name)
        if number == 0:
            form_onsite()
        if number < passing:
            continue
        for s in range(1, STEPS):
            for at_side, pair in enumerate((final[s][:2], final[s][2:])):
                if (s, at_side) not in formed and arrived >= names(pair[0]) | names(pair[1]):
                    assemble(sides.at[s, at_side], *parts_of(pair[0]), *parts_of(pair[1]))
                    formed.add((s, at_side))
            if s not in formed and {(s, 0), (s, 1)} <= formed:
                multiply(s, sides.at[s, 0], sides.at[s, 1])
                formed.add(s)
    for leg in legs:
        when(leg.sends, r, c, copies[leg.name].wait_send)


def shards(u_blocks, u_rows):
    legs, final = plan()
    count = len(OWN) + len(legs)
    return pl.pallas_call(
        functools.partial(kernel, legs, final),
        out_shape=pltpu.VMEM((STEPS, TAU, TAU, BS, BS), jnp.float32),
        in_specs=[pl.BlockSpec(memory_space=pltpu.HBM)] * 2,
        out_specs=pl.BlockSpec(memory_space=pltpu.VMEM),
        scratch_shapes=[
            pltpu.VMEM((count, TAU, HEIGHT, BS), jnp.float32),
            pltpu.VMEM((TAU, BS, BS), jnp.float32),
            pltpu.SMEM((TAU, 2 * STEPS - 1), jnp.int32),
            pltpu.VMEM((STEPS, 2, 2, TAU * BS, TAU * BS), jnp.bfloat16),
            pltpu.SemaphoreType.DMA,
            pltpu.SemaphoreType.DMA((2 * STEPS - 1, TAU)),
            pltpu.SemaphoreType.DMA((len(legs),)),
            pltpu.SemaphoreType.DMA((len(legs),)),
        ],
        compiler_params=pltpu.CompilerParams(collective_id=0, has_side_effects=True, vmem_limit_bytes=40 << 20),
    )(*(pltpu.with_memory_space_constraint(each, pltpu.HBM) for each in (u_blocks, u_rows)))


def solution(mesh):
    return jax.shard_map(
        shards,
        mesh=mesh,
        in_specs=(P("row", "col", None, None), P("row", "col")),
        out_specs=P("row", "col", None, None, None),
        check_vma=False,
    )
```

profile of v0, /device:TPU:56, one launch (start us, length us, event | category | flops | bytes accessed | tf_op | source)
XLA Modules:
  0.0 92.5 jit_solution(15999277624309889876)
XLA Ops:
  0.0 91.1 %shard_map.28 = f32[4,3,3,128,128]{4,3,2,1,0:T(8,128)S(1)} custom-call(f32[3,7,128,128]{3,2,1,0:T(8,128)} %u_ref.1, s32[3,7]{1,0:T(4,128)} %rows_hbm.1), custom_call_target="tpu_custom_call" | custom-call | tf_op jit(solution)/shard_map/pallas_call | solution.py:266
  91.1 1.4 %copy.4 = f32[4,3,3,128,128]{4,3,2,1,0:T(8,128)} copy(f32[4,3,3,128,128]{4,3,2,1,0:T(8,128)S(1)} %shard_map.28) | data formatting | bytes 4718592
where the time goes:
time: 92.7 us; the launch traced here: 92.5 us
  Pallas kernels  91.1 us (98%)
  local copies, waits for them, and re-layouts  1.41 us (2%)
    pallas_call x1, Pallas kernels, shards(): pl.pallas_call(functools.partial(kernel, legs, final), out_shape=pltpu.VM...  91.1 us

commit v1 on v0

--- a/solution.py
+++ b/solution.py
@@ -105,10 +105,10 @@
 
 
 ORDER = (
-    "n1", "n1z", "fe1", "p2", "f3", "f2", "bs3", "fe1z", "fm1", "fe2", "fe2z", "fe3", "bm2", "c1", "bs2", "bm1",
-    "fm3", "bm2z", "fm1z", "bs1", "fm2", "fm2x", "bs2z", "bm3",
+    "n1", "p2", "f3", "n1z", "fe1", "fm1", "f2", "fe2", "bs3", "fe2z", "bm2", "fe3", "c1", "fm1z", "bs2", "fe1z",
+    "bm3", "bm1", "bm2z", "bs1", "fm2", "fm2x", "fm3", "bs2z",
 )
-AFTER = {"bm2": "n1", "c1": "f2", "fe2": "fe1", "fm3": "f2", "p2": "n1"}
+AFTER = {"bm2": "n1", "bs2z": "fm1", "bs3": "n1", "c1": "f2", "fe2": "fm1", "fm3": "f2"}
 
 
 OWN = ["F1", "F2", "F3", "B1", "B2", "B3"]

time: 92.7 us -> 88.3 us (0.953)
  the two profiles are of different devices: /device:TPU:56 before, /device:TPU:214 now
where the time goes in v1:
time: 88.3 us; the launch traced here: 88.1 us
  Pallas kernels  86.7 us (98%)
  local copies, waits for them, and re-layouts  1.41 us (2%)
    pallas_call x1, Pallas kernels, shards(): pl.pallas_call(functools.partial(kernel, legs, final), out_shape=pltpu.VM...  86.7 us

profile of v1, /device:TPU:214, one launch (start us, length us, event | category | flops | bytes accessed | tf_op | source)
XLA Modules:
  0.0 88.1 jit_solution(12280748288373911080)
XLA Ops:
  0.0 86.7 %shard_map.28 = f32[4,3,3,128,128]{4,3,2,1,0:T(8,128)S(1)} custom-call(f32[3,7,128,128]{3,2,1,0:T(8,128)} %u_ref.1, s32[3,7]{1,0:T(4,128)} %rows_hbm.1), custom_call_target="tpu_custom_call" | custom-call | tf_op jit(solution)/shard_map/pallas_call | solution.py:266
  86.7 1.4 %copy.4 = f32[4,3,3,128,128]{4,3,2,1,0:T(8,128)} copy(f32[4,3,3,128,128]{4,3,2,1,0:T(8,128)S(1)} %shard_map.28) | data formatting | bytes 4718592

commit v2 on v1

--- a/solution.py
+++ b/solution.py
@@ -78,7 +78,7 @@
     leg("f3", "F3", straight(RING, 0), low(6))
     leg("fe3", (low(6), "f3", "F3"), in_plane(6, 0))
     leg("fm3", (low(3), "f3", "F3"), in_row_plane(3, 3))
-    bs3 = leg("bs3", "B3", straight(0, 6))
+    bs3 = late("bs3", "B3", 0, 6)
     leg("bm3", bs3, straight(3, -3))
     final[3] = "fm3", bs3, "fe3", "bm3"
 
@@ -105,10 +105,10 @@
 
 
 ORDER = (
-    "n1", "p2", "f3", "n1z", "fe1", "fm1", "f2", "fe2", "bs3", "fe2z", "bm2", "fe3", "c1", "fm1z", "bs2", "fe1z",
-    "bm3", "bm1", "bm2z", "bs1", "fm2", "fm2x", "fm3", "bs2z",
+    "n1", "n1z", "p2", "fe1", "fe1z", "f3", "f2", "bs3", "fm1", "bs3z", "fe2", "fe2z", "bm2", "c1", "bs2", "fe3",
+    "bm1", "fm3", "bs1", "fm2", "fm2x", "bm3", "fm1z", "bm2z", "bs2z",
 )
-AFTER = {"bm2": "n1", "bs2z": "fm1", "bs3": "n1", "c1": "f2", "fe2": "fm1", "fm3": "f2"}
+AFTER = {"bm2": "n1", "c1": "bs3", "f2": "n1", "f3": "n1", "fe2": "n1", "fm3": "f2", "p2": "n1"}
 
 
 OWN = ["F1", "F2", "F3", "B1", "B2", "B3"]

time: 88.3 us -> 84.9 us (0.961)
  the two profiles are of different devices: /device:TPU:214 before, /device:TPU:181 now
where the time goes in v2:
time: 84.9 us; the launch traced here: 84.7 us
  Pallas kernels  83.3 us (98%)
  local copies, waits for them, and re-layouts  1.41 us (2%)
    pallas_call x1, Pallas kernels, shards(): pl.pallas_call(functools.partial(kernel, legs, final), out_shape=pltpu.VM...  83.3 us

profile of v2, /device:TPU:181, one launch (start us, length us, event | category | flops | bytes accessed | tf_op | source)
XLA Modules:
  0.0 84.7 jit_solution(15404552220646920913)
XLA Ops:
  0.0 83.3 %shard_map.28 = f32[4,3,3,128,128]{4,3,2,1,0:T(8,128)S(1)} custom-call(f32[3,7,128,128]{3,2,1,0:T(8,128)} %u_ref.1, s32[3,7]{1,0:T(4,128)} %rows_hbm.1), custom_call_target="tpu_custom_call" | custom-call | tf_op jit(solution)/shard_map/pallas_call | solution.py:266
  83.3 1.4 %copy.4 = f32[4,3,3,128,128]{4,3,2,1,0:T(8,128)} copy(f32[4,3,3,128,128]{4,3,2,1,0:T(8,128)S(1)} %shard_map.28) | data formatting | bytes 4718592

commit v3 on v2

--- a/solution.py
+++ b/solution.py
@@ -168,20 +168,24 @@
         when(leg.gets, r, c, greet)
         partners += 1 if leg.sends is None else jnp.where(leg.sends(r, c), 1, 0)
 
-    loads = [pltpu.make_async_copy(rows_hbm, rows_ref, rows_sem)]
-    loads[0].start()
-    for j in range(2 * STEPS - 1):
+    labels_load = pltpu.make_async_copy(rows_hbm, rows_ref, rows_sem)
+    labels_load.start()
+    loads = {}
+    for j in (1, 6, 2, 3, 5, 4, 0):
+        loads[j] = []
         for t in range(TAU):
             target = onsite.at[t] if j == 0 else buf.at[j - 1, t, pl.ds(0, BS)]
-            loads.append(pltpu.make_async_copy(u_ref.at[t, j], target, load_sem.at[j, t]))
-            loads[-1].start()
-    loads[0].wait()
+            loads[j].append(pltpu.make_async_copy(u_ref.at[t, j], target, load_sem.at[j, t]))
+            loads[j][-1].start()
+    labels_load.wait()
     for j in range(1, 2 * STEPS - 1):
         for t in range(TAU):
             buf[j - 1, t, BS:HEIGHT, :] = jnp.full((HEIGHT - BS, BS), rows_ref[t, j], jnp.int32).astype(jnp.float32)
-    for load in loads[1:]:
-        load.wait()
     pl.semaphore_wait(barrier, partners)
+
+    def loaded(j):
+        for load in loads.pop(j, ()):
+            load.wait()
 
     rank = {None: -1, **{leg.name: number for number, leg in enumerate(legs)}}
 
@@ -191,6 +195,10 @@
     def begin(event):
         for leg in legs:
             go = copies[leg.name].start
+            if event is None:
+                own = leg.src if isinstance(leg.src, str) else leg.src[2]
+                if own in OWN and trigger(leg, own) is None:
+                    loaded(1 + OWN.index(own))
             if isinstance(leg.src, str):
                 if event == trigger(leg, leg.src):
                     when(leg.sends, r, c, go)
@@ -202,6 +210,8 @@
                     when(lambda r, c: jnp.logical_not(condition(r, c)), r, c, go)
 
     begin(None)
+    for j in list(loads):
+        loaded(j)
 
     def put(side, i, k, value):
         high, low = split(value)

time: 84.9 us -> 84.9 us (level)
  no operation moved by 1% of the time
where the time goes in v3:
time: 84.9 us; the launch traced here: 84.7 us
  Pallas kernels  83.3 us (98%)
  local copies, waits for them, and re-layouts  1.41 us (2%)
    pallas_call x1, Pallas kernels, shards(): pl.pallas_call(functools.partial(kernel, legs, final), out_shape=pltpu.VM...  83.3 us

profile of v3, /device:TPU:181, one launch (start us, length us, event | category | flops | bytes accessed | tf_op | source)
XLA Modules:
  0.0 84.7 jit_solution(4254179447049658094)
XLA Ops:
  0.0 83.3 %shard_map.28 = f32[4,3,3,128,128]{4,3,2,1,0:T(8,128)S(1)} custom-call(f32[3,7,128,128]{3,2,1,0:T(8,128)} %u_ref.1, s32[3,7]{1,0:T(4,128)} %rows_hbm.1), custom_call_target="tpu_custom_call" | custom-call | tf_op jit(solution)/shard_map/pallas_call | solution.py:276
  83.3 1.4 %copy.4 = f32[4,3,3,128,128]{4,3,2,1,0:T(8,128)} copy(f32[4,3,3,128,128]{4,3,2,1,0:T(8,128)S(1)} %shard_map.28) | data formatting | bytes 4718592
